TPU v7x, 128 devices: a whole 4x4x4 slice. The times are simulated.
128 devices in a mesh: item: 8 (over x_lo, z), user: 16 (over x_hi, y, core).
Axes of the slice: x: 4 (x_hi: 2, x_lo: 2; x = x_hi * 2 + x_lo), y: 4, z: 4, core: 2. Of those that a mesh axis runs over, the one named last changes fastest.
Arguments:
- history: bfloat16 [128, 1024, 512], P(('item', 'user')), may hold values from -6 to 6
- hist_len: int32 [128], P(('item', 'user')), may hold values from 256 to 1024, as said below
- cand_ids: int32 [128, 128], P(('item', 'user')), may hold values from 0 to 383, as said below
- cand_lists: int32 [128, 4], P(('item', 'user')), may hold values from 0 to 15, as said below
- item_table: bfloat16 [6144, 512], P('user', 'item'), may hold values from -6 to 6
- w_in: bfloat16 [512, 2048], replicated, may hold values from -0.25 to 0.25
- w_out: bfloat16 [512, 512], replicated, may hold values from -0.25 to 0.25
- grad_cand: bfloat16 [128, 128, 512], P(('item', 'user')), may hold values from -6 to 6
Outputs:
- hist_out: bfloat16 [128, 1024, 512], P(('item', 'user'))
- cand_out: bfloat16 [128, 128, 512], P(('item', 'user'))
- table_grad: float32 [6144, 512], P('user', 'item')
Inputs may be any that keep to these rules, and one draw needn't show every extreme that they name: `hist_len`: some user has exactly 1024 events; positions at or past a user's length are padding. `cand_ids`: the 128 ids of one user are different. `cand_lists`: the 4 entries of user g are different and none equals g mod 16.
All inputs are finite; a program needn't handle non-finite values.
Results may differ from a plain program's by a relative error of at most 0.013.
Values may be sent and summed in bfloat16 or wider, within the bound.
A program may use at most 64 MiB of HBM per device.

v0:
```python
import jax
import jax.numpy as jnp
from jax import lax
from jax.sharding import PartitionSpec as P

H = 8
NORM_EPS = 1e-05


def from_behind(block, axis, distance):
    devices = range(lax.axis_size(axis))
    route = [((i - distance) % len(devices), i) for i in devices]
    return lax.ppermute(block, axis, route)


def silu_slope(pre_act):
    sigmoid = jax.nn.sigmoid(pre_act)
    return sigmoid * (1.0 + pre_act * (1.0 - sigmoid))


def normalize(rows_in):
    centred = rows_in - jnp.mean(rows_in, axis=-1, keepdims=True)
    inv_dev = lax.rsqrt(jnp.mean(centred * centred, axis=-1, keepdims=True) + NORM_EPS)
    return (centred * inv_dev, inv_dev)


def history_layer(events, length, projected, w_out):
    event_rows = events.shape[0]
    model_width = events.shape[1]
    head_size = model_width // H
    att_scale = head_size ** (-0.5)
    block_rows = min(512, event_rows)
    u_part = projected[:, :model_width]
    heads_v = projected[:, model_width : 2 * model_width].reshape(event_rows, H, head_size)
    heads_q = projected[:, 2 * model_width : 3 * model_width].reshape(event_rows, H, head_size)
    heads_k = projected[:, 3 * model_width :].reshape(event_rows, H, head_size)
    block_total = (length + block_rows - 1) // block_rows

    def query_block(q_index, result):
        q_start = q_index * block_rows
        q_tile = lax.dynamic_slice_in_dim(heads_q, q_start, block_rows, 0)
        q_pos = q_start + jnp.arange(block_rows)

        def key_block(k_index, running):
            k_start = k_index * block_rows
            k_tile = lax.dynamic_slice_in_dim(heads_k, k_start, block_rows, 0)
            v_tile = lax.dynamic_slice_in_dim(heads_v, k_start, block_rows, 0)
            k_pos = k_start + jnp.arange(block_rows)
            scores = (
                jnp.einsum("qhd,khd->hqk", q_tile, k_tile, preferred_element_type=jnp.float32)
                * att_scale
            )
            allowed = (k_pos[None, :] <= q_pos[:, None]) & (k_pos[None, :] < length)
            weights = jnp.where(allowed[None], jax.nn.silu(scores), 0.0).astype(jnp.bfloat16)
            return running + jnp.einsum(
                "hqk,khd->qhd", weights, v_tile, preferred_element_type=jnp.float32
            )

        attended = lax.fori_loop(
            0, q_index + 1, key_block, jnp.zeros((block_rows, H, head_size), jnp.float32)
        )
        normed = normalize(attended.reshape(block_rows, model_width))[0]
        u_tile = lax.dynamic_slice_in_dim(u_part, q_start, block_rows, 0)
        mixed_rows = (normed * u_tile.astype(jnp.float32)).astype(jnp.bfloat16)
        x_tile = lax.dynamic_slice_in_dim(events, q_start, block_rows, 0)
        layer_out = jnp.dot(mixed_rows, w_out, preferred_element_type=jnp.float32) + x_tile.astype(
            jnp.float32
        )
        layer_out = jnp.where((q_pos < length)[:, None], layer_out, 0.0).astype(jnp.bfloat16)
        return lax.dynamic_update_slice_in_dim(result, layer_out, q_start, 0)

    return lax.fori_loop(0, block_total, query_block, jnp.zeros_like(events))


def candidate_pass(
    cand_q, cand_u, cand_emb, keys_k, keys_v, valid_keys, skip_rows, w_out, grad_rows
):
    cand_rows = cand_q.shape[0]
    model_width = cand_q.shape[1]
    head_size = model_width // H
    att_scale = head_size ** (-0.5)
    heads_q = cand_q.reshape(cand_rows, H, head_size)
    heads_k = keys_k.reshape(-1, H, head_size)
    heads_v = keys_v.reshape(-1, H, head_size)
    scores = (
        jnp.einsum("qhd,khd->hqk", heads_q, heads_k, preferred_element_type=jnp.float32) * att_scale
    )
    weights = jnp.where(valid_keys[None, None, :], jax.nn.silu(scores), 0.0).astype(jnp.bfloat16)
    attended = jnp.einsum(
        "hqk,khd->qhd", weights, heads_v, preferred_element_type=jnp.float32
    ).reshape(cand_rows, model_width)
    normed, inv_dev = normalize(attended)
    u_rows = cand_u.astype(jnp.float32)
    mixed_rows = (normed * u_rows).astype(jnp.bfloat16)
    layer_out = (
        jnp.dot(mixed_rows, w_out, preferred_element_type=jnp.float32)
        + cand_emb.astype(jnp.float32)
    ).astype(jnp.bfloat16)
    grad_mixed = jnp.einsum("rd,ed->re", grad_rows, w_out, preferred_element_type=jnp.float32)
    grad_u = grad_mixed * normed
    grad_normed = grad_mixed * u_rows
    grad_att = inv_dev * (
        grad_normed
        - jnp.mean(grad_normed, axis=-1, keepdims=True)
        - normed * jnp.mean(grad_normed * normed, axis=-1, keepdims=True)
    )
    grad_att = grad_att.astype(jnp.bfloat16).reshape(cand_rows, H, head_size)
    grad_weights = jnp.einsum("qhd,khd->hqk", grad_att, heads_v, preferred_element_type=jnp.float32)
    grad_scores = (
        jnp.where(valid_keys[None, None, :], grad_weights * silu_slope(scores), 0.0) * att_scale
    ).astype(jnp.bfloat16)
    grad_q = jnp.einsum(
        "hqk,khd->qhd", grad_scores, heads_k, preferred_element_type=jnp.float32
    ).reshape(cand_rows, model_width)
    grad_k = jnp.einsum(
        "hqk,qhd->khd", grad_scores[:, :, skip_rows:], heads_q, preferred_element_type=jnp.float32
    ).reshape(-1, model_width)
    grad_v = jnp.einsum(
        "hqk,qhd->khd", weights[:, :, skip_rows:], grad_att, preferred_element_type=jnp.float32
    ).reshape(-1, model_width)
    return (layer_out, grad_u, grad_q, grad_k, grad_v)


def local(history, hist_len, cand_ids, cand_lists, item_table, w_in, w_out, grad_cand):
    events = history[0]
    length = hist_len[0]
    own_ids = cand_ids[0]
    my_lists = cand_lists[0]
    grad_rows = grad_cand[0]
    event_rows = events.shape[0]
    model_width = events.shape[1]
    cand_count = own_ids.shape[0]
    slot_count = my_lists.shape[0]
    part_rows = item_table.shape[0]
    cycle_size = lax.axis_size("user")
    cycle_pos = lax.axis_index("user")
    catalogue = jnp.arange(part_rows, dtype=jnp.int32)
    own_hot = (own_ids[:, None] == catalogue[None, :]).astype(jnp.bfloat16)
    cand_emb = jnp.dot(
        own_hot,
        lax.all_gather(item_table, "item", axis=1, tiled=True),
        preferred_element_type=jnp.float32,
    ).astype(jnp.bfloat16)
    projected = jax.nn.silu(jnp.dot(events, w_in, preferred_element_type=jnp.float32)).astype(
        jnp.bfloat16
    )
    cand_pre = jnp.dot(cand_emb, w_in, preferred_element_type=jnp.float32)
    cand_proj = jax.nn.silu(cand_pre).astype(jnp.bfloat16)
    cand_u = cand_proj[:, :model_width]
    cand_v = cand_proj[:, model_width : 2 * model_width]
    cand_q = cand_proj[:, 2 * model_width : 3 * model_width]
    cand_k = cand_proj[:, 3 * model_width :]
    block_kv = jnp.concatenate([cand_k, cand_v], 1)
    held_slots = jnp.zeros((slot_count, cand_count, 2 * model_width), jnp.bfloat16)

    def store_block(slots_now, moving, source):
        return jnp.where((my_lists == source)[:, None, None], moving[None], slots_now)

    def forward_turn(turn_no, carried):
        moving, slots_now = carried
        moving = from_behind(moving, "user", 1)
        return (moving, store_block(slots_now, moving, (cycle_pos - turn_no) % cycle_size))

    held_slots = lax.fori_loop(1, cycle_size, forward_turn, (block_kv, held_slots))[1]
    hist_out = history_layer(events, length, projected, w_out)
    slot_k = held_slots[:, :, :model_width].reshape(slot_count * cand_count, model_width)
    slot_v = held_slots[:, :, model_width:].reshape(slot_count * cand_count, model_width)
    keys_k = jnp.concatenate([projected[:, 3 * model_width :], cand_k, slot_k], 0)
    keys_v = jnp.concatenate([projected[:, model_width : 2 * model_width], cand_v, slot_v], 0)
    valid_keys = jnp.concatenate(
        [jnp.arange(event_rows) < length, jnp.ones(((1 + slot_count) * cand_count,), dtype=bool)], 0
    )
    cand_out, grad_u, grad_q, grad_k, grad_v = candidate_pass(
        cand_q, cand_u, cand_emb, keys_k, keys_v, valid_keys, event_rows, w_out, grad_rows
    )
    grad_own = jnp.concatenate([grad_k[:cand_count], grad_v[:cand_count]], 1)
    grad_slots = jnp.concatenate(
        [
            grad_k[cand_count:].reshape(slot_count, cand_count, model_width),
            grad_v[cand_count:].reshape(slot_count, cand_count, model_width),
        ],
        2,
    )

    def slot_terms(owner):
        matched = my_lists == owner % cycle_size
        return jnp.sum(jnp.where(matched[:, None, None], grad_slots, 0.0), 0)

    def give_back(turn_no, running):
        running = from_behind(running.astype(jnp.bfloat16), "user", 1).astype(running.dtype)
        return running + slot_terms(cycle_pos - turn_no)

    grad_home = lax.fori_loop(1, cycle_size + 1, give_back, grad_own)
    grad_proj = jnp.concatenate(
        [grad_u, grad_home[:, model_width:], grad_q, grad_home[:, :model_width]], 1
    )
    grad_pre = (grad_proj * silu_slope(cand_pre)).astype(jnp.bfloat16)
    grad_emb = jnp.einsum(
        "rf,df->rd", grad_pre, w_in, preferred_element_type=jnp.float32
    ) + grad_rows.astype(jnp.float32)
    table_terms = jnp.einsum(
        "cv,cd->vd", own_hot.astype(jnp.float32), grad_emb, precision=lax.Precision.HIGHEST
    )
    table_grad = lax.psum_scatter(
        table_terms.astype(jnp.bfloat16), "item", scatter_dimension=1, tiled=True
    ).astype(jnp.float32)
    return (hist_out[None], cand_out[None], table_grad)


def solution(mesh):
    in_specs = (
        P(("item", "user"), None, None),
        P(("item", "user")),
        P(("item", "user"), None),
        P(("item", "user"), None),
        P("user", "item"),
        P(),
        P(),
        P(("item", "user"), None, None),
    )
    out_specs = (
        P(("item", "user"), None, None),
        P(("item", "user"), None, None),
        P("user", "item"),
    )
    return jax.shard_map(local, mesh=mesh, in_specs=in_specs, out_specs=out_specs, check_vma=False)
```

profile of v0, /device:TPU:0, one launch (start us, length us, event | category | flops | bytes accessed | tf_op | source)
XLA Modules:
  0.0 472.5 jit_solution(8002575875772738989)
XLA Ops:
  7.2 30.4 %all_gather.3 = bf16[384,512]{0,1:T(8,128)(2,1)S(1)} all-gather(bf16[384,64]{0,1:T(8,128)(2,1)} %param.20), channel_id=1, replica_groups=mesh['item'=8,'user'=16] {'item'}, dimensions={1}, use_global_device_ids=true | all-gather | bytes 442368 | tf_op jit(solution)/shard_map/all_gather | solution.py:141
  55.5 161.5 %while.57 = (s32[]{:T(128)}, bf16[128,1024]{1,0:T(8,128)(2,1)}, bf16[4,128,1024]{2,1,0:T(8,128)(2,1)S(1)}, s32[]{:T(128)}, s32[4]{0:T(128)S(1)}, /*index=5*/s32[]{:T(128)}, s32[]{:T(128)}, s32[]{:T(128)}, s32[]{:T(128)}) while((s32[]{:T(128)}, bf16[128,1024]{1,0:T(8,128)(2,1)}, bf16[4,128,1024]{2,1,0:T(8,128)(2,1)S(1)}, s32[]{:T(128)}, ...), condition=%wide.region_7.8_spmd.clone, body=%wide.region_6.7_spmd.clone.sunk | while | flops 1048595 | bytes 3932460 | solution.py:164
  55.5 9.6 %collective-permute-done.1 = bf16[128,1024]{1,0:T(8,128)(2,1)S(1)} collective-permute-done((bf16[128,1024]{1,0:T(8,128)(2,1)}, bf16[128,1024]{1,0:T(8,128)(2,1)S(1)}, u32[]{:S(2)}, u32[]{:S(2)}) %collective-permute-start.1) | collective-permute-done | bytes 262176 | tf_op jit(solution)/shard_map/while/body/eval_jaxpr/ppermute | solution.py:13
  66.4 9.6 %collective-permute-done.1 = bf16[128,1024]{1,0:T(8,128)(2,1)S(1)} collective-permute-done((bf16[128,1024]{1,0:T(8,128)(2,1)}, bf16[128,1024]{1,0:T(8,128)(2,1)S(1)}, u32[]{:S(2)}, u32[]{:S(2)}) %collective-permute-start.1) | collective-permute-done | bytes 262176 | tf_op jit(solution)/shard_map/while/body/eval_jaxpr/ppermute | solution.py:13
  77.1 9.6 %collective-permute-done.1 = bf16[128,1024]{1,0:T(8,128)(2,1)S(1)} collective-permute-done((bf16[128,1024]{1,0:T(8,128)(2,1)}, bf16[128,1024]{1,0:T(8,128)(2,1)S(1)}, u32[]{:S(2)}, u32[]{:S(2)}) %collective-permute-start.1) | collective-permute-done | bytes 262176 | tf_op jit(solution)/shard_map/while/body/eval_jaxpr/ppermute | solution.py:13
  87.9 9.6 %collective-permute-done.1 = bf16[128,1024]{1,0:T(8,128)(2,1)S(1)} collective-permute-done((bf16[128,1024]{1,0:T(8,128)(2,1)}, bf16[128,1024]{1,0:T(8,128)(2,1)S(1)}, u32[]{:S(2)}, u32[]{:S(2)}) %collective-permute-start.1) | collective-permute-done | bytes 262176 | tf_op jit(solution)/shard_map/while/body/eval_jaxpr/ppermute | solution.py:13
  98.7 9.6 %collective-permute-done.1 = bf16[128,1024]{1,0:T(8,128)(2,1)S(1)} collective-permute-done((bf16[128,1024]{1,0:T(8,128)(2,1)}, bf16[128,1024]{1,0:T(8,128)(2,1)S(1)}, u32[]{:S(2)}, u32[]{:S(2)}) %collective-permute-start.1) | collective-permute-done | bytes 262176 | tf_op jit(solution)/shard_map/while/body/eval_jaxpr/ppermute | solution.py:13
  109.5 9.6 %collective-permute-done.1 = bf16[128,1024]{1,0:T(8,128)(2,1)S(1)} collective-permute-done((bf16[128,1024]{1,0:T(8,128)(2,1)}, bf16[128,1024]{1,0:T(8,128)(2,1)S(1)}, u32[]{:S(2)}, u32[]{:S(2)}) %collective-permute-start.1) | collective-permute-done | bytes 262176 | tf_op jit(solution)/shard_map/while/body/eval_jaxpr/ppermute | solution.py:13
  120.2 9.6 %collective-permute-done.1 = bf16[128,1024]{1,0:T(8,128)(2,1)S(1)} collective-permute-done((bf16[128,1024]{1,0:T(8,128)(2,1)}, bf16[128,1024]{1,0:T(8,128)(2,1)S(1)}, u32[]{:S(2)}, u32[]{:S(2)}) %collective-permute-start.1) | collective-permute-done | bytes 262176 | tf_op jit(solution)/shard_map/while/body/eval_jaxpr/ppermute | solution.py:13
  131.0 9.6 %collective-permute-done.1 = bf16[128,1024]{1,0:T(8,128)(2,1)S(1)} collective-permute-done((bf16[128,1024]{1,0:T(8,128)(2,1)}, bf16[128,1024]{1,0:T(8,128)(2,1)S(1)}, u32[]{:S(2)}, u32[]{:S(2)}) %collective-permute-start.1) | collective-permute-done | bytes 262176 | tf_op jit(solution)/shard_map/while/body/eval_jaxpr/ppermute | solution.py:13
  141.8 9.6 %collective-permute-done.1 = bf16[128,1024]{1,0:T(8,128)(2,1)S(1)} collective-permute-done((bf16[128,1024]{1,0:T(8,128)(2,1)}, bf16[128,1024]{1,0:T(8,128)(2,1)S(1)}, u32[]{:S(2)}, u32[]{:S(2)}) %collective-permute-start.1) | collective-permute-done | bytes 262176 | tf_op jit(solution)/shard_map/while/body/eval_jaxpr/ppermute | solution.py:13
  152.5 9.6 %collective-permute-done.1 = bf16[128,1024]{1,0:T(8,128)(2,1)S(1)} collective-permute-done((bf16[128,1024]{1,0:T(8,128)(2,1)}, bf16[128,1024]{1,0:T(8,128)(2,1)S(1)}, u32[]{:S(2)}, u32[]{:S(2)}) %collective-permute-start.1) | collective-permute-done | bytes 262176 | tf_op jit(solution)/shard_map/while/body/eval_jaxpr/ppermute | solution.py:13
  163.3 9.6 %collective-permute-done.1 = bf16[128,1024]{1,0:T(8,128)(2,1)S(1)} collective-permute-done((bf16[128,1024]{1,0:T(8,128)(2,1)}, bf16[128,1024]{1,0:T(8,128)(2,1)S(1)}, u32[]{:S(2)}, u32[]{:S(2)}) %collective-permute-start.1) | collective-permute-done | bytes 262176 | tf_op jit(solution)/shard_map/while/body/eval_jaxpr/ppermute | solution.py:13
  174.1 9.6 %collective-permute-done.1 = bf16[128,1024]{1,0:T(8,128)(2,1)S(1)} collective-permute-done((bf16[128,1024]{1,0:T(8,128)(2,1)}, bf16[128,1024]{1,0:T(8,128)(2,1)S(1)}, u32[]{:S(2)}, u32[]{:S(2)}) %collective-permute-start.1) | collective-permute-done | bytes 262176 | tf_op jit(solution)/shard_map/while/body/eval_jaxpr/ppermute | solution.py:13
  184.9 9.6 %collective-permute-done.1 = bf16[128,1024]{1,0:T(8,128)(2,1)S(1)} collective-permute-done((bf16[128,1024]{1,0:T(8,128)(2,1)}, bf16[128,1024]{1,0:T(8,128)(2,1)S(1)}, u32[]{:S(2)}, u32[]{:S(2)}) %collective-permute-start.1) | collective-permute-done | bytes 262176 | tf_op jit(solution)/shard_map/while/body/eval_jaxpr/ppermute | solution.py:13
  195.6 9.6 %collective-permute-done.1 = bf16[128,1024]{1,0:T(8,128)(2,1)S(1)} collective-permute-done((bf16[128,1024]{1,0:T(8,128)(2,1)}, bf16[128,1024]{1,0:T(8,128)(2,1)S(1)}, u32[]{:S(2)}, u32[]{:S(2)}) %collective-permute-start.1) | collective-permute-done | bytes 262176 | tf_op jit(solution)/shard_map/while/body/eval_jaxpr/ppermute | solution.py:13
  206.4 9.6 %collective-permute-done.1 = bf16[128,1024]{1,0:T(8,128)(2,1)S(1)} collective-permute-done((bf16[128,1024]{1,0:T(8,128)(2,1)}, bf16[128,1024]{1,0:T(8,128)(2,1)S(1)}, u32[]{:S(2)}, u32[]{:S(2)}) %collective-permute-start.1) | collective-permute-done | bytes 262176 | tf_op jit(solution)/shard_map/while/body/eval_jaxpr/ppermute | solution.py:13
  261.9 153.9 %while.56 = (s32[]{:T(128)}, f32[128,1024]{1,0:T(8,128)S(1)}, s32[]{:T(128)}, s32[4]{0:T(128)S(1)}, f32[4,128,1024]{2,1,0:T(8,128)}, /*index=5*/s32[]{:T(128)}, s32[]{:T(128)}, s32[]{:T(128)}, s32[]{:T(128)}) while((s32[]{:T(128)}, f32[128,1024]{1,0:T(8,128)S(1)}, s32[]{:T(128)}, s32[4]{0:T(128)S(1)}, f32[4,128,1024]{2,1,0:T(8,128)}, ...), condition=%wide.region_14.15_spmd, body=%wide.region_12.14_spmd.sunk | while | flops 1310738 | bytes 5767450 | solution.py:193
  264.0 7.4 %collective-permute-done = bf16[128,1024]{1,0:T(8,128)(2,1)S(1)} collective-permute-done((bf16[128,1024]{1,0:T(8,128)(2,1)S(1)}, bf16[128,1024]{1,0:T(8,128)(2,1)S(1)}, u32[]{:S(2)}, u32[]{:S(2)}) %collective-permute-start) | collective-permute-done | bytes 262176 | tf_op jit(solution)/shard_map/while/body/eval_jaxpr/ppermute | solution.py:13
  283.2 7.4 %collective-permute-done = bf16[128,1024]{1,0:T(8,128)(2,1)S(1)} collective-permute-done((bf16[128,1024]{1,0:T(8,128)(2,1)S(1)}, bf16[128,1024]{1,0:T(8,128)(2,1)S(1)}, u32[]{:S(2)}, u32[]{:S(2)}) %collective-permute-start) | collective-permute-done | bytes 262176 | tf_op jit(solution)/shard_map/while/body/eval_jaxpr/ppermute | solution.py:13
  292.8 7.4 %collective-permute-done = bf16[128,1024]{1,0:T(8,128)(2,1)S(1)} collective-permute-done((bf16[128,1024]{1,0:T(8,128)(2,1)S(1)}, bf16[128,1024]{1,0:T(8,128)(2,1)S(1)}, u32[]{:S(2)}, u32[]{:S(2)}) %collective-permute-start) | collective-permute-done | bytes 262176 | tf_op jit(solution)/shard_map/while/body/eval_jaxpr/ppermute | solution.py:13
  302.5 7.4 %collective-permute-done = bf16[128,1024]{1,0:T(8,128)(2,1)S(1)} collective-permute-done((bf16[128,1024]{1,0:T(8,128)(2,1)S(1)}, bf16[128,1024]{1,0:T(8,128)(2,1)S(1)}, u32[]{:S(2)}, u32[]{:S(2)}) %collective-permute-start) | collective-permute-done | bytes 262176 | tf_op jit(solution)/shard_map/while/body/eval_jaxpr/ppermute | solution.py:13
  423.7 38.3 %while.55 = (s32[]{:T(128)}, bf16[1024,512]{1,0:T(8,128)(2,1)}, s32[]{:T(128)}, s32[]{:T(128)}, bf16[1024,8,64]{0,2,1:T(8,128)(2,1)}, /*index=5*/bf16[1024,8,64]...) while((s32[]{:T(128)}, bf16[1024,512]{1,0:T(8,128)(2,1)}, ...), condition=%wide.region_5.6_spmd, body=%wide.region_0.5_spmd.sunk | while | flops 824184320 | bytes 14710306 | solution.py:72
  442.1 11.3 %while.58 = (s32[]{:T(128)}, f32[512,8,64]{0,2,1:T(8,128)S(1)}, s32[]{:T(128)}, bf16[1024,8,64]{0,2,1:T(8,128)(2,1)}, s32[]{:T(128)}, /*index=5*/bf16[1024,8,64]...) while((s32[]{:T(128)}, f32[512,8,64]{0,2,1:T(8,128)S(1)}, ...), condition=%wide.region_2.2_spmd.clone, body=%wide.region_1.1_spmd.clone.sunk | while | flops 552339456 | bytes 4204731 | solution.py:59
  (303 shorter events, 257.1 us)
Async XLA Ops:
  7.2 457.0 %reduce-scatter.2.cloned.1.call-start = ((), (), s32[]{:S(2)}) async-start(), calls=%async_computation.1 | async-start | bytes 442368 | tf_op jit(solution)/shard_map/reduce_scatter | solution.py:204
  55.5 9.6 %collective-permute-start.1 = (bf16[128,1024]{1,0:T(8,128)(2,1)}, bf16[128,1024]{1,0:T(8,128)(2,1)S(1)}, u32[]{:S(2)}, u32[]{:S(2)}) collective-permute-start(bf16[128,1024]{1,0:T(8,128)(2,1)} %get-tuple-element.808), channel_id=1, source_target_pairs={{15,0},{0,1},{1,2},{2,3},{3,4},{4,5},{5,6},{6,7},{7,8},{8,9},{9,10... | collective-permute-start | bytes 786440 | tf_op jit(solution)/shard_map/while/body/eval_jaxpr/ppermute | solution.py:13
  66.2 9.7 %collective-permute-start.1 = (bf16[128,1024]{1,0:T(8,128)(2,1)}, bf16[128,1024]{1,0:T(8,128)(2,1)S(1)}, u32[]{:S(2)}, u32[]{:S(2)}) collective-permute-start(bf16[128,1024]{1,0:T(8,128)(2,1)} %get-tuple-element.808), channel_id=1, source_target_pairs={{15,0},{0,1},{1,2},{2,3},{3,4},{4,5},{5,6},{6,7},{7,8},{8,9},{9,10... | collective-permute-start | bytes 786440 | tf_op jit(solution)/shard_map/while/body/eval_jaxpr/ppermute | solution.py:13
  77.0 9.7 %collective-permute-start.1 = (bf16[128,1024]{1,0:T(8,128)(2,1)}, bf16[128,1024]{1,0:T(8,128)(2,1)S(1)}, u32[]{:S(2)}, u32[]{:S(2)}) collective-permute-start(bf16[128,1024]{1,0:T(8,128)(2,1)} %get-tuple-element.808), channel_id=1, source_target_pairs={{15,0},{0,1},{1,2},{2,3},{3,4},{4,5},{5,6},{6,7},{7,8},{8,9},{9,10... | collective-permute-start | bytes 786440 | tf_op jit(solution)/shard_map/while/body/eval_jaxpr/ppermute | solution.py:13
  87.8 9.7 %collective-permute-start.1 = (bf16[128,1024]{1,0:T(8,128)(2,1)}, bf16[128,1024]{1,0:T(8,128)(2,1)S(1)}, u32[]{:S(2)}, u32[]{:S(2)}) collective-permute-start(bf16[128,1024]{1,0:T(8,128)(2,1)} %get-tuple-element.808), channel_id=1, source_target_pairs={{15,0},{0,1},{1,2},{2,3},{3,4},{4,5},{5,6},{6,7},{7,8},{8,9},{9,10... | collective-permute-start | bytes 786440 | tf_op jit(solution)/shard_map/while/body/eval_jaxpr/ppermute | solution.py:13
  98.6 9.7 %collective-permute-start.1 = (bf16[128,1024]{1,0:T(8,128)(2,1)}, bf16[128,1024]{1,0:T(8,128)(2,1)S(1)}, u32[]{:S(2)}, u32[]{:S(2)}) collective-permute-start(bf16[128,1024]{1,0:T(8,128)(2,1)} %get-tuple-element.808), channel_id=1, source_target_pairs={{15,0},{0,1},{1,2},{2,3},{3,4},{4,5},{5,6},{6,7},{7,8},{8,9},{9,10... | collective-permute-start | bytes 786440 | tf_op jit(solution)/shard_map/while/body/eval_jaxpr/ppermute | solution.py:13
  109.3 9.7 %collective-permute-start.1 = (bf16[128,1024]{1,0:T(8,128)(2,1)}, bf16[128,1024]{1,0:T(8,128)(2,1)S(1)}, u32[]{:S(2)}, u32[]{:S(2)}) collective-permute-start(bf16[128,1024]{1,0:T(8,128)(2,1)} %get-tuple-element.808), channel_id=1, source_target_pairs={{15,0},{0,1},{1,2},{2,3},{3,4},{4,5},{5,6},{6,7},{7,8},{8,9},{9,10... | collective-permute-start | bytes 786440 | tf_op jit(solution)/shard_map/while/body/eval_jaxpr/ppermute | solution.py:13
  120.1 9.7 %collective-permute-start.1 = (bf16[128,1024]{1,0:T(8,128)(2,1)}, bf16[128,1024]{1,0:T(8,128)(2,1)S(1)}, u32[]{:S(2)}, u32[]{:S(2)}) collective-permute-start(bf16[128,1024]{1,0:T(8,128)(2,1)} %get-tuple-element.808), channel_id=1, source_target_pairs={{15,0},{0,1},{1,2},{2,3},{3,4},{4,5},{5,6},{6,7},{7,8},{8,9},{9,10... | collective-permute-start | bytes 786440 | tf_op jit(solution)/shard_map/while/body/eval_jaxpr/ppermute | solution.py:13
  130.9 9.7 %collective-permute-start.1 = (bf16[128,1024]{1,0:T(8,128)(2,1)}, bf16[128,1024]{1,0:T(8,128)(2,1)S(1)}, u32[]{:S(2)}, u32[]{:S(2)}) collective-permute-start(bf16[128,1024]{1,0:T(8,128)(2,1)} %get-tuple-element.808), channel_id=1, source_target_pairs={{15,0},{0,1},{1,2},{2,3},{3,4},{4,5},{5,6},{6,7},{7,8},{8,9},{9,10... | collective-permute-start | bytes 786440 | tf_op jit(solution)/shard_map/while/body/eval_jaxpr/ppermute | solution.py:13
  141.7 9.7 %collective-permute-start.1 = (bf16[128,1024]{1,0:T(8,128)(2,1)}, bf16[128,1024]{1,0:T(8,128)(2,1)S(1)}, u32[]{:S(2)}, u32[]{:S(2)}) collective-permute-start(bf16[128,1024]{1,0:T(8,128)(2,1)} %get-tuple-element.808), channel_id=1, source_target_pairs={{15,0},{0,1},{1,2},{2,3},{3,4},{4,5},{5,6},{6,7},{7,8},{8,9},{9,10... | collective-permute-start | bytes 786440 | tf_op jit(solution)/shard_map/while/body/eval_jaxpr/ppermute | solution.py:13
  152.4 9.7 %collective-permute-start.1 = (bf16[128,1024]{1,0:T(8,128)(2,1)}, bf16[128,1024]{1,0:T(8,128)(2,1)S(1)}, u32[]{:S(2)}, u32[]{:S(2)}) collective-permute-start(bf16[128,1024]{1,0:T(8,128)(2,1)} %get-tuple-element.808), channel_id=1, source_target_pairs={{15,0},{0,1},{1,2},{2,3},{3,4},{4,5},{5,6},{6,7},{7,8},{8,9},{9,10... | collective-permute-start | bytes 786440 | tf_op jit(solution)/shard_map/while/body/eval_jaxpr/ppermute | solution.py:13
  163.2 9.7 %collective-permute-start.1 = (bf16[128,1024]{1,0:T(8,128)(2,1)}, bf16[128,1024]{1,0:T(8,128)(2,1)S(1)}, u32[]{:S(2)}, u32[]{:S(2)}) collective-permute-start(bf16[128,1024]{1,0:T(8,128)(2,1)} %get-tuple-element.808), channel_id=1, source_target_pairs={{15,0},{0,1},{1,2},{2,3},{3,4},{4,5},{5,6},{6,7},{7,8},{8,9},{9,10... | collective-permute-start | bytes 786440 | tf_op jit(solution)/shard_map/while/body/eval_jaxpr/ppermute | solution.py:13
  174.0 9.7 %collective-permute-start.1 = (bf16[128,1024]{1,0:T(8,128)(2,1)}, bf16[128,1024]{1,0:T(8,128)(2,1)S(1)}, u32[]{:S(2)}, u32[]{:S(2)}) collective-permute-start(bf16[128,1024]{1,0:T(8,128)(2,1)} %get-tuple-element.808), channel_id=1, source_target_pairs={{15,0},{0,1},{1,2},{2,3},{3,4},{4,5},{5,6},{6,7},{7,8},{8,9},{9,10... | collective-permute-start | bytes 786440 | tf_op jit(solution)/shard_map/while/body/eval_jaxpr/ppermute | solution.py:13
  184.7 9.7 %collective-permute-start.1 = (bf16[128,1024]{1,0:T(8,128)(2,1)}, bf16[128,1024]{1,0:T(8,128)(2,1)S(1)}, u32[]{:S(2)}, u32[]{:S(2)}) collective-permute-start(bf16[128,1024]{1,0:T(8,128)(2,1)} %get-tuple-element.808), channel_id=1, source_target_pairs={{15,0},{0,1},{1,2},{2,3},{3,4},{4,5},{5,6},{6,7},{7,8},{8,9},{9,10... | collective-permute-start | bytes 786440 | tf_op jit(solution)/shard_map/while/body/eval_jaxpr/ppermute | solution.py:13
  195.5 9.7 %collective-permute-start.1 = (bf16[128,1024]{1,0:T(8,128)(2,1)}, bf16[128,1024]{1,0:T(8,128)(2,1)S(1)}, u32[]{:S(2)}, u32[]{:S(2)}) collective-permute-start(bf16[128,1024]{1,0:T(8,128)(2,1)} %get-tuple-element.808), channel_id=1, source_target_pairs={{15,0},{0,1},{1,2},{2,3},{3,4},{4,5},{5,6},{6,7},{7,8},{8,9},{9,10... | collective-permute-start | bytes 786440 | tf_op jit(solution)/shard_map/while/body/eval_jaxpr/ppermute | solution.py:13
  206.3 9.7 %collective-permute-start.1 = (bf16[128,1024]{1,0:T(8,128)(2,1)}, bf16[128,1024]{1,0:T(8,128)(2,1)S(1)}, u32[]{:S(2)}, u32[]{:S(2)}) collective-permute-start(bf16[128,1024]{1,0:T(8,128)(2,1)} %get-tuple-element.808), channel_id=1, source_target_pairs={{15,0},{0,1},{1,2},{2,3},{3,4},{4,5},{5,6},{6,7},{7,8},{8,9},{9,10... | collective-permute-start | bytes 786440 | tf_op jit(solution)/shard_map/while/body/eval_jaxpr/ppermute | solution.py:13
  262.0 9.5 %collective-permute-start = (bf16[128,1024]{1,0:T(8,128)(2,1)S(1)}, bf16[128,1024]{1,0:T(8,128)(2,1)S(1)}, u32[]{:S(2)}, u32[]{:S(2)}) collective-permute-start(bf16[128,1024]{1,0:T(8,128)(2,1)S(1)} %convert_element_type.146), channel_id=1, source_target_pairs={{15,0},{0,1},{1,2},{2,3},{3,4},{4,5},{5,6},{6,7},{7,8},{8,9},{9,10... | collective-permute-start | bytes 786440 | tf_op jit(solution)/shard_map/while/body/eval_jaxpr/ppermute | solution.py:13
  271.6 9.5 %collective-permute-start = (bf16[128,1024]{1,0:T(8,128)(2,1)S(1)}, bf16[128,1024]{1,0:T(8,128)(2,1)S(1)}, u32[]{:S(2)}, u32[]{:S(2)}) collective-permute-start(bf16[128,1024]{1,0:T(8,128)(2,1)S(1)} %convert_element_type.146), channel_id=1, source_target_pairs={{15,0},{0,1},{1,2},{2,3},{3,4},{4,5},{5,6},{6,7},{7,8},{8,9},{9,10... | collective-permute-start | bytes 786440 | tf_op jit(solution)/shard_map/while/body/eval_jaxpr/ppermute | solution.py:13
  281.2 9.5 %collective-permute-start = (bf16[128,1024]{1,0:T(8,128)(2,1)S(1)}, bf16[128,1024]{1,0:T(8,128)(2,1)S(1)}, u32[]{:S(2)}, u32[]{:S(2)}) collective-permute-start(bf16[128,1024]{1,0:T(8,128)(2,1)S(1)} %convert_element_type.146), channel_id=1, source_target_pairs={{15,0},{0,1},{1,2},{2,3},{3,4},{4,5},{5,6},{6,7},{7,8},{8,9},{9,10... | collective-permute-start | bytes 786440 | tf_op jit(solution)/shard_map/while/body/eval_jaxpr/ppermute | solution.py:13
  290.8 9.5 %collective-permute-start = (bf16[128,1024]{1,0:T(8,128)(2,1)S(1)}, bf16[128,1024]{1,0:T(8,128)(2,1)S(1)}, u32[]{:S(2)}, u32[]{:S(2)}) collective-permute-start(bf16[128,1024]{1,0:T(8,128)(2,1)S(1)} %convert_element_type.146), channel_id=1, source_target_pairs={{15,0},{0,1},{1,2},{2,3},{3,4},{4,5},{5,6},{6,7},{7,8},{8,9},{9,10... | collective-permute-start | bytes 786440 | tf_op jit(solution)/shard_map/while/body/eval_jaxpr/ppermute | solution.py:13
  300.4 9.5 %collective-permute-start = (bf16[128,1024]{1,0:T(8,128)(2,1)S(1)}, bf16[128,1024]{1,0:T(8,128)(2,1)S(1)}, u32[]{:S(2)}, u32[]{:S(2)}) collective-permute-start(bf16[128,1024]{1,0:T(8,128)(2,1)S(1)} %convert_element_type.146), channel_id=1, source_target_pairs={{15,0},{0,1},{1,2},{2,3},{3,4},{4,5},{5,6},{6,7},{7,8},{8,9},{9,10... | collective-permute-start | bytes 786440 | tf_op jit(solution)/shard_map/while/body/eval_jaxpr/ppermute | solution.py:13
  310.0 9.5 %collective-permute-start = (bf16[128,1024]{1,0:T(8,128)(2,1)S(1)}, bf16[128,1024]{1,0:T(8,128)(2,1)S(1)}, u32[]{:S(2)}, u32[]{:S(2)}) collective-permute-start(bf16[128,1024]{1,0:T(8,128)(2,1)S(1)} %convert_element_type.146), channel_id=1, source_target_pairs={{15,0},{0,1},{1,2},{2,3},{3,4},{4,5},{5,6},{6,7},{7,8},{8,9},{9,10... | collective-permute-start | bytes 786440 | tf_op jit(solution)/shard_map/while/body/eval_jaxpr/ppermute | solution.py:13
  319.6 9.5 %collective-permute-start = (bf16[128,1024]{1,0:T(8,128)(2,1)S(1)}, bf16[128,1024]{1,0:T(8,128)(2,1)S(1)}, u32[]{:S(2)}, u32[]{:S(2)}) collective-permute-start(bf16[128,1024]{1,0:T(8,128)(2,1)S(1)} %convert_element_type.146), channel_id=1, source_target_pairs={{15,0},{0,1},{1,2},{2,3},{3,4},{4,5},{5,6},{6,7},{7,8},{8,9},{9,10... | collective-permute-start | bytes 786440 | tf_op jit(solution)/shard_map/while/body/eval_jaxpr/ppermute | solution.py:13
  329.2 9.5 %collective-permute-start = (bf16[128,1024]{1,0:T(8,128)(2,1)S(1)}, bf16[128,1024]{1,0:T(8,128)(2,1)S(1)}, u32[]{:S(2)}, u32[]{:S(2)}) collective-permute-start(bf16[128,1024]{1,0:T(8,128)(2,1)S(1)} %convert_element_type.146), channel_id=1, source_target_pairs={{15,0},{0,1},{1,2},{2,3},{3,4},{4,5},{5,6},{6,7},{7,8},{8,9},{9,10... | collective-permute-start | bytes 786440 | tf_op jit(solution)/shard_map/while/body/eval_jaxpr/ppermute | solution.py:13
  (39 other events, 633.5 us)
Sparse Core Ops, SparseCore 0:
  421.4 36.3 reduce-scatter.1
where the time goes:
time: 474 us; the launch traced here: 472 us
  waiting for transfers between devices  262 us (55%)
  local copies, waits for them, and re-layouts  54.7 us (12%)
  other arithmetic  53.8 us (11%)
  matrix products  51.6 us (11%)
  blocking collectives  30.4 us (6%)
  between operations  15.1 us (3%)
    ppermute x31, waiting for transfers between devices, from_behind(): return lax.ppermute(block, axis, route)  262 us
    reduce_sum x16, other arithmetic, slot_terms(): return jnp.sum(jnp.where(matched[:, None, None], grad_slots, 0.0), 0)  31.2 us
    all_gather x1, blocking collectives, local(): lax.all_gather(item_table, 'item', axis=1, tiled=True)  30.4 us
    dot_general x3, matrix products, key_block(): jnp.einsum('hqk,khd->qhd', weights, v_tile, preferred_element_type=jnp.fl...  14 us
    while x15, local copies, waits for them, and re-layouts  10.5 us
  transfers between devices with their start and end apart: 32, of which 31 were waited for; matrix products, arithmetic and copies ran while one was open for 16% of the time, Pallas kernels for 0%

commit v1 on v0

--- a/solution.py
+++ b/solution.py
@@ -138,7 +138,12 @@
     own_hot = (own_ids[:, None] == catalogue[None, :]).astype(jnp.bfloat16)
     cand_emb = jnp.dot(
         own_hot,
-        lax.all_gather(item_table, "item", axis=1, tiled=True),
+        jnp.concatenate(
+            lax.all_to_all(
+                jnp.stack([item_table for _ in range(lax.axis_size("item"))]), "item", 0, 0
+            ),
+            axis=1,
+        ),
         preferred_element_type=jnp.float32,
     ).astype(jnp.bfloat16)
     projected = jax.nn.silu(jnp.dot(events, w_in, preferred_element_type=jnp.float32)).astype(

time: 474 us -> 451 us (0.951)
  blocking collectives: 30.4 us -> 0 us
  starting transfers between devices: 2.27 us -> 8.6 us
    all_gather x1 -> x0, blocking collectives: 30.4 us -> none  [local(): lax.all_gather(item_table, 'item', axis=1, tiled=True)]
    all_to_all x0 -> x1, starting transfers between devices: none -> 6.32 us  [local(): lax.all_to_all(jnp.stack([item_table for _ in range(lax.axis_size('item')...]
  transfers between devices with their start and end apart: 32 -> 33, of which waited for: 31 -> 31; matrix products, arithmetic and copies ran while one was open for 16% -> 19% of each run, Pallas kernels for 0% -> 0%
where the time goes in v1:
time: 451 us; the launch traced here: 449 us
  waiting for transfers between devices  262 us (58%)
  local copies, waits for them, and re-layouts  56.1 us (12%)
  other arithmetic  53.9 us (12%)
  matrix products  50.6 us (11%)
  between operations  15.1 us (3%)
  starting transfers between devices  8.6 us (2%)
    ppermute x31, waiting for transfers between devices, from_behind(): return lax.ppermute(block, axis, route)  262 us
    reduce_sum x16, other arithmetic, slot_terms(): return jnp.sum(jnp.where(matched[:, None, None], grad_slots, 0.0), 0)  31.2 us
    dot_general x3, matrix products, key_block(): jnp.einsum('hqk,khd->qhd', weights, v_tile, preferred_element_type=jnp.fl...  14 us
    while x15, local copies, waits for them, and re-layouts  10.6 us
  transfers between devices with their start and end apart: 33, of which 31 were waited for; matrix products, arithmetic and copies ran while one was open for 19% of the time, Pallas kernels for 0%

profile of v1, /device:TPU:0, one launch (start us, length us, event | category | flops | bytes accessed | tf_op | source)
XLA Modules:
  0.0 448.6 jit_solution(15856531150567395559)
XLA Ops:
  34.8 161.6 %while.57 = (s32[]{:T(128)}, bf16[128,1024]{1,0:T(8,128)(2,1)}, bf16[4,128,1024]{2,1,0:T(8,128)(2,1)S(1)}, s32[]{:T(128)}, s32[4]{0:T(128)S(1)}, /*index=5*/s32[]{:T(128)}, s32[]{:T(128)}, s32[]{:T(128)}, s32[]{:T(128)}) while((s32[]{:T(128)}, bf16[128,1024]{1,0:T(8,128)(2,1)}, bf16[4,128,1024]{2,1,0:T(8,128)(2,1)S(1)}, s32[]{:T(128)}, ...), condition=%wide.region_7.8_spmd.clone, body=%wide.region_6.7_spmd.clone.sunk | while | flops 1048595 | bytes 3932460 | solution.py:169
  34.8 9.6 %collective-permute-done.1 = bf16[128,1024]{1,0:T(8,128)(2,1)S(1)} collective-permute-done((bf16[128,1024]{1,0:T(8,128)(2,1)}, bf16[128,1024]{1,0:T(8,128)(2,1)S(1)}, u32[]{:S(2)}, u32[]{:S(2)}) %collective-permute-start.1) | collective-permute-done | bytes 262176 | tf_op jit(solution)/shard_map/while/body/eval_jaxpr/ppermute | solution.py:13
  45.6 9.6 %collective-permute-done.1 = bf16[128,1024]{1,0:T(8,128)(2,1)S(1)} collective-permute-done((bf16[128,1024]{1,0:T(8,128)(2,1)}, bf16[128,1024]{1,0:T(8,128)(2,1)S(1)}, u32[]{:S(2)}, u32[]{:S(2)}) %collective-permute-start.1) | collective-permute-done | bytes 262176 | tf_op jit(solution)/shard_map/while/body/eval_jaxpr/ppermute | solution.py:13
  56.4 9.6 %collective-permute-done.1 = bf16[128,1024]{1,0:T(8,128)(2,1)S(1)} collective-permute-done((bf16[128,1024]{1,0:T(8,128)(2,1)}, bf16[128,1024]{1,0:T(8,128)(2,1)S(1)}, u32[]{:S(2)}, u32[]{:S(2)}) %collective-permute-start.1) | collective-permute-done | bytes 262176 | tf_op jit(solution)/shard_map/while/body/eval_jaxpr/ppermute | solution.py:13
  67.2 9.6 %collective-permute-done.1 = bf16[128,1024]{1,0:T(8,128)(2,1)S(1)} collective-permute-done((bf16[128,1024]{1,0:T(8,128)(2,1)}, bf16[128,1024]{1,0:T(8,128)(2,1)S(1)}, u32[]{:S(2)}, u32[]{:S(2)}) %collective-permute-start.1) | collective-permute-done | bytes 262176 | tf_op jit(solution)/shard_map/while/body/eval_jaxpr/ppermute | solution.py:13
  78.0 9.6 %collective-permute-done.1 = bf16[128,1024]{1,0:T(8,128)(2,1)S(1)} collective-permute-done((bf16[128,1024]{1,0:T(8,128)(2,1)}, bf16[128,1024]{1,0:T(8,128)(2,1)S(1)}, u32[]{:S(2)}, u32[]{:S(2)}) %collective-permute-start.1) | collective-permute-done | bytes 262176 | tf_op jit(solution)/shard_map/while/body/eval_jaxpr/ppermute | solution.py:13
  88.7 9.6 %collective-permute-done.1 = bf16[128,1024]{1,0:T(8,128)(2,1)S(1)} collective-permute-done((bf16[128,1024]{1,0:T(8,128)(2,1)}, bf16[128,1024]{1,0:T(8,128)(2,1)S(1)}, u32[]{:S(2)}, u32[]{:S(2)}) %collective-permute-start.1) | collective-permute-done | bytes 262176 | tf_op jit(solution)/shard_map/while/body/eval_jaxpr/ppermute | solution.py:13
  99.5 9.6 %collective-permute-done.1 = bf16[128,1024]{1,0:T(8,128)(2,1)S(1)} collective-permute-done((bf16[128,1024]{1,0:T(8,128)(2,1)}, bf16[128,1024]{1,0:T(8,128)(2,1)S(1)}, u32[]{:S(2)}, u32[]{:S(2)}) %collective-permute-start.1) | collective-permute-done | bytes 262176 | tf_op jit(solution)/shard_map/while/body/eval_jaxpr/ppermute | solution.py:13
  110.3 9.6 %collective-permute-done.1 = bf16[128,1024]{1,0:T(8,128)(2,1)S(1)} collective-permute-done((bf16[128,1024]{1,0:T(8,128)(2,1)}, bf16[128,1024]{1,0:T(8,128)(2,1)S(1)}, u32[]{:S(2)}, u32[]{:S(2)}) %collective-permute-start.1) | collective-permute-done | bytes 262176 | tf_op jit(solution)/shard_map/while/body/eval_jaxpr/ppermute | solution.py:13
  121.1 9.6 %collective-permute-done.1 = bf16[128,1024]{1,0:T(8,128)(2,1)S(1)} collective-permute-done((bf16[128,1024]{1,0:T(8,128)(2,1)}, bf16[128,1024]{1,0:T(8,128)(2,1)S(1)}, u32[]{:S(2)}, u32[]{:S(2)}) %collective-permute-start.1) | collective-permute-done | bytes 262176 | tf_op jit(solution)/shard_map/while/body/eval_jaxpr/ppermute | solution.py:13
  131.8 9.6 %collective-permute-done.1 = bf16[128,1024]{1,0:T(8,128)(2,1)S(1)} collective-permute-done((bf16[128,1024]{1,0:T(8,128)(2,1)}, bf16[128,1024]{1,0:T(8,128)(2,1)S(1)}, u32[]{:S(2)}, u32[]{:S(2)}) %collective-permute-start.1) | collective-permute-done | bytes 262176 | tf_op jit(solution)/shard_map/while/body/eval_jaxpr/ppermute | solution.py:13
  142.6 9.6 %collective-permute-done.1 = bf16[128,1024]{1,0:T(8,128)(2,1)S(1)} collective-permute-done((bf16[128,1024]{1,0:T(8,128)(2,1)}, bf16[128,1024]{1,0:T(8,128)(2,1)S(1)}, u32[]{:S(2)}, u32[]{:S(2)}) %collective-permute-start.1) | collective-permute-done | bytes 262176 | tf_op jit(solution)/shard_map/while/body/eval_jaxpr/ppermute | solution.py:13
  153.4 9.6 %collective-permute-done.1 = bf16[128,1024]{1,0:T(8,128)(2,1)S(1)} collective-permute-done((bf16[128,1024]{1,0:T(8,128)(2,1)}, bf16[128,1024]{1,0:T(8,128)(2,1)S(1)}, u32[]{:S(2)}, u32[]{:S(2)}) %collective-permute-start.1) | collective-permute-done | bytes 262176 | tf_op jit(solution)/shard_map/while/body/eval_jaxpr/ppermute | solution.py:13
  164.2 9.6 %collective-permute-done.1 = bf16[128,1024]{1,0:T(8,128)(2,1)S(1)} collective-permute-done((bf16[128,1024]{1,0:T(8,128)(2,1)}, bf16[128,1024]{1,0:T(8,128)(2,1)S(1)}, u32[]{:S(2)}, u32[]{:S(2)}) %collective-permute-start.1) | collective-permute-done | bytes 262176 | tf_op jit(solution)/shard_map/while/body/eval_jaxpr/ppermute | solution.py:13
  175.0 9.6 %collective-permute-done.1 = bf16[128,1024]{1,0:T(8,128)(2,1)S(1)} collective-permute-done((bf16[128,1024]{1,0:T(8,128)(2,1)}, bf16[128,1024]{1,0:T(8,128)(2,1)S(1)}, u32[]{:S(2)}, u32[]{:S(2)}) %collective-permute-start.1) | collective-permute-done | bytes 262176 | tf_op jit(solution)/shard_map/while/body/eval_jaxpr/ppermute | solution.py:13
  185.7 9.6 %collective-permute-done.1 = bf16[128,1024]{1,0:T(8,128)(2,1)S(1)} collective-permute-done((bf16[128,1024]{1,0:T(8,128)(2,1)}, bf16[128,1024]{1,0:T(8,128)(2,1)S(1)}, u32[]{:S(2)}, u32[]{:S(2)}) %collective-permute-start.1) | collective-permute-done | bytes 262176 | tf_op jit(solution)/shard_map/while/body/eval_jaxpr/ppermute | solution.py:13
  241.4 153.7 %while.56 = (s32[]{:T(128)}, f32[128,1024]{1,0:T(8,128)S(1)}, s32[]{:T(128)}, s32[4]{0:T(128)S(1)}, f32[4,128,1024]{2,1,0:T(8,128)}, /*index=5*/s32[]{:T(128)}, s32[]{:T(128)}, s32[]{:T(128)}, s32[]{:T(128)}) while((s32[]{:T(128)}, f32[128,1024]{1,0:T(8,128)S(1)}, s32[]{:T(128)}, s32[4]{0:T(128)S(1)}, f32[4,128,1024]{2,1,0:T(8,128)}, ...), condition=%wide.region_14.15_spmd, body=%wide.region_12.14_spmd.sunk | while | flops 1310738 | bytes 5767450 | solution.py:198
  243.5 7.4 %collective-permute-done = bf16[128,1024]{1,0:T(8,128)(2,1)S(1)} collective-permute-done((bf16[128,1024]{1,0:T(8,128)(2,1)S(1)}, bf16[128,1024]{1,0:T(8,128)(2,1)S(1)}, u32[]{:S(2)}, u32[]{:S(2)}) %collective-permute-start) | collective-permute-done | bytes 262176 | tf_op jit(solution)/shard_map/while/body/eval_jaxpr/ppermute | solution.py:13
  253.1 7.4 %collective-permute-done = bf16[128,1024]{1,0:T(8,128)(2,1)S(1)} collective-permute-done((bf16[128,1024]{1,0:T(8,128)(2,1)S(1)}, bf16[128,1024]{1,0:T(8,128)(2,1)S(1)}, u32[]{:S(2)}, u32[]{:S(2)}) %collective-permute-start) | collective-permute-done | bytes 262176 | tf_op jit(solution)/shard_map/while/body/eval_jaxpr/ppermute | solution.py:13
  262.7 7.4 %collective-permute-done = bf16[128,1024]{1,0:T(8,128)(2,1)S(1)} collective-permute-done((bf16[128,1024]{1,0:T(8,128)(2,1)S(1)}, bf16[128,1024]{1,0:T(8,128)(2,1)S(1)}, u32[]{:S(2)}, u32[]{:S(2)}) %collective-permute-start) | collective-permute-done | bytes 262176 | tf_op jit(solution)/shard_map/while/body/eval_jaxpr/ppermute | solution.py:13
  272.3 7.4 %collective-permute-done = bf16[128,1024]{1,0:T(8,128)(2,1)S(1)} collective-permute-done((bf16[128,1024]{1,0:T(8,128)(2,1)S(1)}, bf16[128,1024]{1,0:T(8,128)(2,1)S(1)}, u32[]{:S(2)}, u32[]{:S(2)}) %collective-permute-start) | collective-permute-done | bytes 262176 | tf_op jit(solution)/shard_map/while/body/eval_jaxpr/ppermute | solution.py:13
  281.9 7.4 %collective-permute-done = bf16[128,1024]{1,0:T(8,128)(2,1)S(1)} collective-permute-done((bf16[128,1024]{1,0:T(8,128)(2,1)S(1)}, bf16[128,1024]{1,0:T(8,128)(2,1)S(1)}, u32[]{:S(2)}, u32[]{:S(2)}) %collective-permute-start) | collective-permute-done | bytes 262176 | tf_op jit(solution)/shard_map/while/body/eval_jaxpr/ppermute | solution.py:13
  399.8 38.4 %while.55 = (s32[]{:T(128)}, bf16[1024,512]{1,0:T(8,128)(2,1)}, s32[]{:T(128)}, s32[]{:T(128)}, bf16[1024,8,64]{0,2,1:T(8,128)(2,1)}, /*index=5*/bf16[1024,8,64]...) while((s32[]{:T(128)}, bf16[1024,512]{1,0:T(8,128)(2,1)}, ...), condition=%wide.region_5.6_spmd, body=%wide.region_0.5_spmd.sunk | while | flops 824184320 | bytes 14710306 | solution.py:72
  418.2 11.3 %while.58 = (s32[]{:T(128)}, f32[512,8,64]{0,2,1:T(8,128)S(1)}, s32[]{:T(128)}, bf16[1024,8,64]{0,2,1:T(8,128)(2,1)}, s32[]{:T(128)}, /*index=5*/bf16[1024,8,64]...) while((s32[]{:T(128)}, f32[512,8,64]{0,2,1:T(8,128)S(1)}, ...), condition=%wide.region_2.2_spmd.clone, body=%wide.region_1.1_spmd.clone.sunk | while | flops 552339456 | bytes 4204731 | solution.py:59
  (303 shorter events, 256.4 us)
Async XLA Ops:
  8.9 20.3 %all-to-all-start = ((bf16[8,384,64]{1,2,0:T(8,128)(2,1)}), bf16[8,384,64]{1,2,0:T(8,128)(2,1)S(1)}, u32[]{:S(2)}, u32[]{:S(2)}) async-start(bf16[8,384,64]{1,2,0:T(8,128)(2,1)} %stack.2), calls=%async_computation | async-start | bytes 786432 | tf_op jit(solution)/shard_map/all_to_all | solution.py:142
  15.2 425.1 %reduce-scatter.2.cloned.1.call-start = ((), (), s32[]{:S(2)}) async-start(), calls=%async_computation.2 | async-start | bytes 442368 | tf_op jit(solution)/shard_map/reduce_scatter | solution.py:209
  34.8 9.6 %collective-permute-start.1 = (bf16[128,1024]{1,0:T(8,128)(2,1)}, bf16[128,1024]{1,0:T(8,128)(2,1)S(1)}, u32[]{:S(2)}, u32[]{:S(2)}) collective-permute-start(bf16[128,1024]{1,0:T(8,128)(2,1)} %get-tuple-element.808), channel_id=1, source_target_pairs={{15,0},{0,1},{1,2},{2,3},{3,4},{4,5},{5,6},{6,7},{7,8},{8,9},{9,10... | collective-permute-start | bytes 786440 | tf_op jit(solution)/shard_map/while/body/eval_jaxpr/ppermute | solution.py:13
  45.5 9.7 %collective-permute-start.1 = (bf16[128,1024]{1,0:T(8,128)(2,1)}, bf16[128,1024]{1,0:T(8,128)(2,1)S(1)}, u32[]{:S(2)}, u32[]{:S(2)}) collective-permute-start(bf16[128,1024]{1,0:T(8,128)(2,1)} %get-tuple-element.808), channel_id=1, source_target_pairs={{15,0},{0,1},{1,2},{2,3},{3,4},{4,5},{5,6},{6,7},{7,8},{8,9},{9,10... | collective-permute-start | bytes 786440 | tf_op jit(solution)/shard_map/while/body/eval_jaxpr/ppermute | solution.py:13
  56.3 9.7 %collective-permute-start.1 = (bf16[128,1024]{1,0:T(8,128)(2,1)}, bf16[128,1024]{1,0:T(8,128)(2,1)S(1)}, u32[]{:S(2)}, u32[]{:S(2)}) collective-permute-start(bf16[128,1024]{1,0:T(8,128)(2,1)} %get-tuple-element.808), channel_id=1, source_target_pairs={{15,0},{0,1},{1,2},{2,3},{3,4},{4,5},{5,6},{6,7},{7,8},{8,9},{9,10... | collective-permute-start | bytes 786440 | tf_op jit(solution)/shard_map/while/body/eval_jaxpr/ppermute | solution.py:13
  67.1 9.7 %collective-permute-start.1 = (bf16[128,1024]{1,0:T(8,128)(2,1)}, bf16[128,1024]{1,0:T(8,128)(2,1)S(1)}, u32[]{:S(2)}, u32[]{:S(2)}) collective-permute-start(bf16[128,1024]{1,0:T(8,128)(2,1)} %get-tuple-element.808), channel_id=1, source_target_pairs={{15,0},{0,1},{1,2},{2,3},{3,4},{4,5},{5,6},{6,7},{7,8},{8,9},{9,10... | collective-permute-start | bytes 786440 | tf_op jit(solution)/shard_map/while/body/eval_jaxpr/ppermute | solution.py:13
  77.8 9.7 %collective-permute-start.1 = (bf16[128,1024]{1,0:T(8,128)(2,1)}, bf16[128,1024]{1,0:T(8,128)(2,1)S(1)}, u32[]{:S(2)}, u32[]{:S(2)}) collective-permute-start(bf16[128,1024]{1,0:T(8,128)(2,1)} %get-tuple-element.808), channel_id=1, source_target_pairs={{15,0},{0,1},{1,2},{2,3},{3,4},{4,5},{5,6},{6,7},{7,8},{8,9},{9,10... | collective-permute-start | bytes 786440 | tf_op jit(solution)/shard_map/while/body/eval_jaxpr/ppermute | solution.py:13
  88.6 9.7 %collective-permute-start.1 = (bf16[128,1024]{1,0:T(8,128)(2,1)}, bf16[128,1024]{1,0:T(8,128)(2,1)S(1)}, u32[]{:S(2)}, u32[]{:S(2)}) collective-permute-start(bf16[128,1024]{1,0:T(8,128)(2,1)} %get-tuple-element.808), channel_id=1, source_target_pairs={{15,0},{0,1},{1,2},{2,3},{3,4},{4,5},{5,6},{6,7},{7,8},{8,9},{9,10... | collective-permute-start | bytes 786440 | tf_op jit(solution)/shard_map/while/body/eval_jaxpr/ppermute | solution.py:13
  99.4 9.7 %collective-permute-start.1 = (bf16[128,1024]{1,0:T(8,128)(2,1)}, bf16[128,1024]{1,0:T(8,128)(2,1)S(1)}, u32[]{:S(2)}, u32[]{:S(2)}) collective-permute-start(bf16[128,1024]{1,0:T(8,128)(2,1)} %get-tuple-element.808), channel_id=1, source_target_pairs={{15,0},{0,1},{1,2},{2,3},{3,4},{4,5},{5,6},{6,7},{7,8},{8,9},{9,10... | collective-permute-start | bytes 786440 | tf_op jit(solution)/shard_map/while/body/eval_jaxpr/ppermute | solution.py:13
  110.2 9.7 %collective-permute-start.1 = (bf16[128,1024]{1,0:T(8,128)(2,1)}, bf16[128,1024]{1,0:T(8,128)(2,1)S(1)}, u32[]{:S(2)}, u32[]{:S(2)}) collective-permute-start(bf16[128,1024]{1,0:T(8,128)(2,1)} %get-tuple-element.808), channel_id=1, source_target_pairs={{15,0},{0,1},{1,2},{2,3},{3,4},{4,5},{5,6},{6,7},{7,8},{8,9},{9,10... | collective-permute-start | bytes 786440 | tf_op jit(solution)/shard_map/while/body/eval_jaxpr/ppermute | solution.py:13
  121.0 9.7 %collective-permute-start.1 = (bf16[128,1024]{1,0:T(8,128)(2,1)}, bf16[128,1024]{1,0:T(8,128)(2,1)S(1)}, u32[]{:S(2)}, u32[]{:S(2)}) collective-permute-start(bf16[128,1024]{1,0:T(8,128)(2,1)} %get-tuple-element.808), channel_id=1, source_target_pairs={{15,0},{0,1},{1,2},{2,3},{3,4},{4,5},{5,6},{6,7},{7,8},{8,9},{9,10... | collective-permute-start | bytes 786440 | tf_op jit(solution)/shard_map/while/body/eval_jaxpr/ppermute | solution.py:13
  131.7 9.7 %collective-permute-start.1 = (bf16[128,1024]{1,0:T(8,128)(2,1)}, bf16[128,1024]{1,0:T(8,128)(2,1)S(1)}, u32[]{:S(2)}, u32[]{:S(2)}) collective-permute-start(bf16[128,1024]{1,0:T(8,128)(2,1)} %get-tuple-element.808), channel_id=1, source_target_pairs={{15,0},{0,1},{1,2},{2,3},{3,4},{4,5},{5,6},{6,7},{7,8},{8,9},{9,10... | collective-permute-start | bytes 786440 | tf_op jit(solution)/shard_map/while/body/eval_jaxpr/ppermute | solution.py:13
  142.5 9.7 %collective-permute-start.1 = (bf16[128,1024]{1,0:T(8,128)(2,1)}, bf16[128,1024]{1,0:T(8,128)(2,1)S(1)}, u32[]{:S(2)}, u32[]{:S(2)}) collective-permute-start(bf16[128,1024]{1,0:T(8,128)(2,1)} %get-tuple-element.808), channel_id=1, source_target_pairs={{15,0},{0,1},{1,2},{2,3},{3,4},{4,5},{5,6},{6,7},{7,8},{8,9},{9,10... | collective-permute-start | bytes 786440 | tf_op jit(solution)/shard_map/while/body/eval_jaxpr/ppermute | solution.py:13
  153.3 9.7 %collective-permute-start.1 = (bf16[128,1024]{1,0:T(8,128)(2,1)}, bf16[128,1024]{1,0:T(8,128)(2,1)S(1)}, u32[]{:S(2)}, u32[]{:S(2)}) collective-permute-start(bf16[128,1024]{1,0:T(8,128)(2,1)} %get-tuple-element.808), channel_id=1, source_target_pairs={{15,0},{0,1},{1,2},{2,3},{3,4},{4,5},{5,6},{6,7},{7,8},{8,9},{9,10... | collective-permute-start | bytes 786440 | tf_op jit(solution)/shard_map/while/body/eval_jaxpr/ppermute | solution.py:13
  164.1 9.7 %collective-permute-start.1 = (bf16[128,1024]{1,0:T(8,128)(2,1)}, bf16[128,1024]{1,0:T(8,128)(2,1)S(1)}, u32[]{:S(2)}, u32[]{:S(2)}) collective-permute-start(bf16[128,1024]{1,0:T(8,128)(2,1)} %get-tuple-element.808), channel_id=1, source_target_pairs={{15,0},{0,1},{1,2},{2,3},{3,4},{4,5},{5,6},{6,7},{7,8},{8,9},{9,10... | collective-permute-start | bytes 786440 | tf_op jit(solution)/shard_map/while/body/eval_jaxpr/ppermute | solution.py:13
  174.8 9.7 %collective-permute-start.1 = (bf16[128,1024]{1,0:T(8,128)(2,1)}, bf16[128,1024]{1,0:T(8,128)(2,1)S(1)}, u32[]{:S(2)}, u32[]{:S(2)}) collective-permute-start(bf16[128,1024]{1,0:T(8,128)(2,1)} %get-tuple-element.808), channel_id=1, source_target_pairs={{15,0},{0,1},{1,2},{2,3},{3,4},{4,5},{5,6},{6,7},{7,8},{8,9},{9,10... | collective-permute-start | bytes 786440 | tf_op jit(solution)/shard_map/while/body/eval_jaxpr/ppermute | solution.py:13
  185.6 9.7 %collective-permute-start.1 = (bf16[128,1024]{1,0:T(8,128)(2,1)}, bf16[128,1024]{1,0:T(8,128)(2,1)S(1)}, u32[]{:S(2)}, u32[]{:S(2)}) collective-permute-start(bf16[128,1024]{1,0:T(8,128)(2,1)} %get-tuple-element.808), channel_id=1, source_target_pairs={{15,0},{0,1},{1,2},{2,3},{3,4},{4,5},{5,6},{6,7},{7,8},{8,9},{9,10... | collective-permute-start | bytes 786440 | tf_op jit(solution)/shard_map/while/body/eval_jaxpr/ppermute | solution.py:13
  241.4 9.5 %collective-permute-start = (bf16[128,1024]{1,0:T(8,128)(2,1)S(1)}, bf16[128,1024]{1,0:T(8,128)(2,1)S(1)}, u32[]{:S(2)}, u32[]{:S(2)}) collective-permute-start(bf16[128,1024]{1,0:T(8,128)(2,1)S(1)} %convert_element_type.146), channel_id=1, source_target_pairs={{15,0},{0,1},{1,2},{2,3},{3,4},{4,5},{5,6},{6,7},{7,8},{8,9},{9,10... | collective-permute-start | bytes 786440 | tf_op jit(solution)/shard_map/while/body/eval_jaxpr/ppermute | solution.py:13
  251.0 9.5 %collective-permute-start = (bf16[128,1024]{1,0:T(8,128)(2,1)S(1)}, bf16[128,1024]{1,0:T(8,128)(2,1)S(1)}, u32[]{:S(2)}, u32[]{:S(2)}) collective-permute-start(bf16[128,1024]{1,0:T(8,128)(2,1)S(1)} %convert_element_type.146), channel_id=1, source_target_pairs={{15,0},{0,1},{1,2},{2,3},{3,4},{4,5},{5,6},{6,7},{7,8},{8,9},{9,10... | collective-permute-start | bytes 786440 | tf_op jit(solution)/shard_map/while/body/eval_jaxpr/ppermute | solution.py:13
  260.6 9.5 %collective-permute-start = (bf16[128,1024]{1,0:T(8,128)(2,1)S(1)}, bf16[128,1024]{1,0:T(8,128)(2,1)S(1)}, u32[]{:S(2)}, u32[]{:S(2)}) collective-permute-start(bf16[128,1024]{1,0:T(8,128)(2,1)S(1)} %convert_element_type.146), channel_id=1, source_target_pairs={{15,0},{0,1},{1,2},{2,3},{3,4},{4,5},{5,6},{6,7},{7,8},{8,9},{9,10... | collective-permute-start | bytes 786440 | tf_op jit(solution)/shard_map/while/body/eval_jaxpr/ppermute | solution.py:13
  270.2 9.5 %collective-permute-start = (bf16[128,1024]{1,0:T(8,128)(2,1)S(1)}, bf16[128,1024]{1,0:T(8,128)(2,1)S(1)}, u32[]{:S(2)}, u32[]{:S(2)}) collective-permute-start(bf16[128,1024]{1,0:T(8,128)(2,1)S(1)} %convert_element_type.146), channel_id=1, source_target_pairs={{15,0},{0,1},{1,2},{2,3},{3,4},{4,5},{5,6},{6,7},{7,8},{8,9},{9,10... | collective-permute-start | bytes 786440 | tf_op jit(solution)/shard_map/while/body/eval_jaxpr/ppermute | solution.py:13
  279.8 9.5 %collective-permute-start = (bf16[128,1024]{1,0:T(8,128)(2,1)S(1)}, bf16[128,1024]{1,0:T(8,128)(2,1)S(1)}, u32[]{:S(2)}, u32[]{:S(2)}) collective-permute-start(bf16[128,1024]{1,0:T(8,128)(2,1)S(1)} %convert_element_type.146), channel_id=1, source_target_pairs={{15,0},{0,1},{1,2},{2,3},{3,4},{4,5},{5,6},{6,7},{7,8},{8,9},{9,10... | collective-permute-start | bytes 786440 | tf_op jit(solution)/shard_map/while/body/eval_jaxpr/ppermute | solution.py:13
  289.4 9.5 %collective-permute-start = (bf16[128,1024]{1,0:T(8,128)(2,1)S(1)}, bf16[128,1024]{1,0:T(8,128)(2,1)S(1)}, u32[]{:S(2)}, u32[]{:S(2)}) collective-permute-start(bf16[128,1024]{1,0:T(8,128)(2,1)S(1)} %convert_element_type.146), channel_id=1, source_target_pairs={{15,0},{0,1},{1,2},{2,3},{3,4},{4,5},{5,6},{6,7},{7,8},{8,9},{9,10... | collective-permute-start | bytes 786440 | tf_op jit(solution)/shard_map/while/body/eval_jaxpr/ppermute | solution.py:13
  299.1 9.5 %collective-permute-start = (bf16[128,1024]{1,0:T(8,128)(2,1)S(1)}, bf16[128,1024]{1,0:T(8,128)(2,1)S(1)}, u32[]{:S(2)}, u32[]{:S(2)}) collective-permute-start(bf16[128,1024]{1,0:T(8,128)(2,1)S(1)} %convert_element_type.146), channel_id=1, source_target_pairs={{15,0},{0,1},{1,2},{2,3},{3,4},{4,5},{5,6},{6,7},{7,8},{8,9},{9,10... | collective-permute-start | bytes 786440 | tf_op jit(solution)/shard_map/while/body/eval_jaxpr/ppermute | solution.py:13
  (39 other events, 618.6 us)
Sparse Core Ops, SparseCore 0:
  398.9 36.6 reduce-scatter.1
